TPU v7x, 512 devices: a whole 4x8x8 slice. The times are simulated.
512 devices in a mesh: row: 32 (over z_lo, y, core), col: 16 (over z_hi, x).
Axes of the slice: x: 4, y: 8, z: 8 (z_hi: 4, z_lo: 2; z = z_hi * 2 + z_lo), core: 2. Of those that a mesh axis runs over, the one named last changes fastest.
Arguments:
- anchors: bfloat16 [65536, 128], P(('row', 'col')), may hold values from -0.7 to 0.7, as said below
- positives: bfloat16 [65536, 128], P(('col', 'row')), may hold values from -0.7 to 0.7, as said below
- row_lse: bfloat16 [65536], P(('row', 'col')), may hold values from 10 to 12
- column_logsumexp: bfloat16 [65536], P(('col', 'row')), may hold values from 10 to 12
Outputs:
- anchor_grad: float32 [65536, 128], P(('row', 'col'))
- matched_partner_derivative: float32 [65536, 128], P(('col', 'row'))
Inputs may be any that keep to these rules, and one draw needn't show every extreme that they name: `anchors`: fingerprint embeddings of recordings in groups of similar ones; each positive is a perturbed copy of its anchor. `positives`: perturbed copies of the anchors.
All inputs are finite; a program needn't handle non-finite values.
Results may differ from a plain program's by a relative error of at most 0.0045.
Values may be sent and summed in bfloat16 or wider, within the bound.
A program may use at most 64 MiB of HBM per device.

v0:
```python
import math

import jax
import jax.numpy as jnp
from jax import lax
from jax.sharding import PartitionSpec as P

sharpness_factor = 10.0
half_inverse = 5.0


def soft_weights(anchor_blk, anchor_lse, positive_blk, positive_lse):
    scores = (
        lax.dot_general(
            anchor_blk, positive_blk, (((1,), (1,)), ((), ())), preferred_element_type=jnp.float32
        )
        * sharpness_factor
    )
    rows_part = jnp.exp(scores - anchor_lse.astype(jnp.float32)[:, None])
    cols_part = jnp.exp(scores - positive_lse.astype(jnp.float32)[None, :])
    return (rows_part + cols_part).astype(jnp.bfloat16)


def aligned(source, offset, batch_extent):
    extent = source.shape[0]
    padded = jnp.pad(source, ((batch_extent, batch_extent), (0, 0)))
    opening = jnp.clip(offset + batch_extent, 0, extent + batch_extent)
    return lax.dynamic_slice_in_dim(padded, opening, batch_extent, 0).astype(jnp.float32)


def block_size(amount):
    return math.gcd(amount, 512)


def on_device(anchors, positives, row_lse, column_logsumexp):
    anchor_rows, anchor_lse = (
        lax.all_gather(anchors, "col", axis=0, tiled=True),
        lax.all_gather(row_lse, "col", axis=0, tiled=True),
    )
    positive_cols, positive_lse = (
        lax.all_gather(positives, "row", axis=0, tiled=True),
        lax.all_gather(column_logsumexp, "row", axis=0, tiled=True),
    )
    tile_rows = anchor_rows.shape[0]
    tile_cols = positive_cols.shape[0]
    features = anchors.shape[1]
    row_root = lax.axis_index("row") * tile_rows
    col_root = lax.axis_index("col") * tile_cols
    row_block = block_size(tile_rows)
    block_list = tile_rows // row_block

    def advance_both(summed, number):
        anchor_blk = lax.dynamic_slice_in_dim(anchor_rows, number * row_block, row_block, 0)
        lse_blk = lax.dynamic_slice_in_dim(anchor_lse, number * row_block, row_block, 0)
        soft = soft_weights(anchor_blk, lse_blk, positive_cols, positive_lse)
        summed = summed + lax.dot_general(
            soft, anchor_blk, (((0,), (0,)), ((), ())), preferred_element_type=jnp.float32
        )
        return (summed, jnp.dot(soft, positive_cols, preferred_element_type=jnp.float32))

    positive_summed, partials = lax.scan(
        advance_both, jnp.zeros((tile_cols, features), jnp.float32), jnp.arange(block_list)
    )
    anchor_local = half_inverse * partials.reshape(tile_rows, features) - 10.0 * aligned(
        positive_cols, row_root - col_root, tile_rows
    )
    matched_partner_shard = half_inverse * positive_summed - 10.0 * aligned(
        anchor_rows, col_root - row_root, tile_cols
    )
    anchor_grad = lax.psum_scatter(anchor_local, "col", scatter_dimension=0, tiled=True)
    matched_partner_derivative = lax.psum_scatter(
        matched_partner_shard, "row", scatter_dimension=0, tiled=True
    )
    return (anchor_grad, matched_partner_derivative)


def solution(mesh):
    return jax.shard_map(
        on_device,
        mesh=mesh,
        in_specs=(
            P(("row", "col"), None),
            P(("col", "row"), None),
            P(("row", "col")),
            P(("col", "row")),
        ),
        out_specs=(P(("row", "col"), None), P(("col", "row"), None)),
        check_vma=False,
    )
```

profile of v0, /device:TPU:1, one launch (start us, length us, event | category | flops | bytes accessed | tf_op | source)
XLA Modules:
  0.0 398.9 jit_solution(3402522471532497670)
XLA Ops:
  7.2 0.7 all-gather.4.cloned.1.call-update
  8.0 42.7 %all-gather = bf16[16,1,128]{2,1,0:T(2,128)(2,1)S(1)} all-gather(bf16[1,1,128]{2,1,0:T(2,128)(2,1)} %bitcast.29), channel_id=1, replica_groups=mesh['row'=32,'col'=16] {'col'}, dimensions={0}, use_global_device_ids=true | all-gather | bytes 4352 | tf_op jit(solution)/shard_map/all_gather | solution.py:38
  50.7 42.4 %all-gather.1 = bf16[32,1,128]{2,1,0:T(2,128)(2,1)S(1)} all-gather(bf16[1,1,128]{2,1,0:T(2,128)(2,1)} %bitcast.30), channel_id=1, replica_groups=mesh['row'=32,'col'=16] {'row'}, dimensions={0}, use_global_device_ids=true | all-gather | bytes 8448 | tf_op jit(solution)/shard_map/all_gather | solution.py:42
  93.2 36.9 %all_gather.12 = bf16[2048,128]{1,0:T(8,128)(2,1)S(1)} all-gather(bf16[128,128]{1,0:T(8,128)(2,1)} %param.6), channel_id=1, replica_groups=mesh['row'=32,'col'=16] {'col'}, dimensions={0}, use_global_device_ids=true | all-gather | bytes 557056 | tf_op jit(solution)/shard_map/all_gather | solution.py:37
  130.1 52.1 %while.13 = (s32[]{:T(128)}, f32[4096,128]{1,0:T(8,128)S(1)}, f32[4,512,128]{2,1,0:T(8,128)}, s32[4]{0:T(128)S(1)}, bf16[2048,128]{1,0:T(8,128)(2,1)S(1)}, /*ind...) while((s32[]{:T(128)}, f32[4096,128]{1,0:T(8,128)S(1)}, ...), condition=%wide.region_1.2_spmd.clone, body=%wide.region_0.1_spmd.clone.sunk | while | flops 1622151680 | bytes 40416520 | solution.py:61
  130.1 0.6 dynamic_slice.39
  131.4 5.4 %add_convert_fusion.2 = bf16[512,4096]{1,0:T(8,128)(2,1)} fusion(bf16[4096,128]{1,0:T(8,128)(2,1)} %get-tuple-element.168, f32[4096]{0:T(1024)S(1)} %convert_element_type.37, f32[512]{0:T(512)S(1)} %dynamic-slice_convert_fusion.2, bf16[2048,128]{1,0:T(8,128)(2,1)S(1)} %get-tuple-element.167, s32[]{:T(128)S(6)} %select_n.8), kind=kOutput, calls=%fused_computation.clone.1 | convolution fusion | flops 547356672 | bytes 5392388 | tf_op jit(solution)/shard_map/while/body/eval_jaxpr/dot_general | solution.py:14
  136.9 4.2 %convolution_add_fusion.2 = f32[4096,128]{1,0:T(8,128)S(1)} fusion(bf16[512,4096]{1,0:T(8,128)(2,1)} %add_convert_fusion.2, f32[4096,128]{1,0:T(8,128)S(1)} %get-tuple-element.152, pred[]{:T(512)S(6)} %compare.5, bf16[2048,128]{1,0:T(8,128)(2,1)S(1)} %get-tuple-element.167, s32[]{:T(128)S(6)} %select_n.8), kind=kOutput, calls=%fused_computation.1.clone.1 | convolution fusion | flops 537919488 | bytes 8519685 | tf_op jit(solution)/shard_map/while/body/eval_jaxpr/dot_general | solution.py:56
  141.1 2.0 fusion.22
  143.1 0.6 dynamic_slice.39
  144.4 5.4 %add_convert_fusion.2 = bf16[512,4096]{1,0:T(8,128)(2,1)} fusion(bf16[4096,128]{1,0:T(8,128)(2,1)} %get-tuple-element.168, f32[4096]{0:T(1024)S(1)} %convert_element_type.37, f32[512]{0:T(512)S(1)} %dynamic-slice_convert_fusion.2, bf16[2048,128]{1,0:T(8,128)(2,1)S(1)} %get-tuple-element.167, s32[]{:T(128)S(6)} %select_n.8), kind=kOutput, calls=%fused_computation.clone.1 | convolution fusion | flops 547356672 | bytes 5392388 | tf_op jit(solution)/shard_map/while/body/eval_jaxpr/dot_general | solution.py:14
  149.9 4.2 %convolution_add_fusion.2 = f32[4096,128]{1,0:T(8,128)S(1)} fusion(bf16[512,4096]{1,0:T(8,128)(2,1)} %add_convert_fusion.2, f32[4096,128]{1,0:T(8,128)S(1)} %get-tuple-element.152, pred[]{:T(512)S(6)} %compare.5, bf16[2048,128]{1,0:T(8,128)(2,1)S(1)} %get-tuple-element.167, s32[]{:T(128)S(6)} %select_n.8), kind=kOutput, calls=%fused_computation.1.clone.1 | convolution fusion | flops 537919488 | bytes 8519685 | tf_op jit(solution)/shard_map/while/body/eval_jaxpr/dot_general | solution.py:56
  154.1 2.0 fusion.22
  157.4 5.4 %add_convert_fusion.2 = bf16[512,4096]{1,0:T(8,128)(2,1)} fusion(bf16[4096,128]{1,0:T(8,128)(2,1)} %get-tuple-element.168, f32[4096]{0:T(1024)S(1)} %convert_element_type.37, f32[512]{0:T(512)S(1)} %dynamic-slice_convert_fusion.2, bf16[2048,128]{1,0:T(8,128)(2,1)S(1)} %get-tuple-element.167, s32[]{:T(128)S(6)} %select_n.8), kind=kOutput, calls=%fused_computation.clone.1 | convolution fusion | flops 547356672 | bytes 5392388 | tf_op jit(solution)/shard_map/while/body/eval_jaxpr/dot_general | solution.py:14
  162.9 4.2 %convolution_add_fusion.2 = f32[4096,128]{1,0:T(8,128)S(1)} fusion(bf16[512,4096]{1,0:T(8,128)(2,1)} %add_convert_fusion.2, f32[4096,128]{1,0:T(8,128)S(1)} %get-tuple-element.152, pred[]{:T(512)S(6)} %compare.5, bf16[2048,128]{1,0:T(8,128)(2,1)S(1)} %get-tuple-element.167, s32[]{:T(128)S(6)} %select_n.8), kind=kOutput, calls=%fused_computation.1.clone.1 | convolution fusion | flops 537919488 | bytes 8519685 | tf_op jit(solution)/shard_map/while/body/eval_jaxpr/dot_general | solution.py:56
  167.2 2.0 fusion.22
  170.5 5.4 %add_convert_fusion.2 = bf16[512,4096]{1,0:T(8,128)(2,1)} fusion(bf16[4096,128]{1,0:T(8,128)(2,1)} %get-tuple-element.168, f32[4096]{0:T(1024)S(1)} %convert_element_type.37, f32[512]{0:T(512)S(1)} %dynamic-slice_convert_fusion.2, bf16[2048,128]{1,0:T(8,128)(2,1)S(1)} %get-tuple-element.167, s32[]{:T(128)S(6)} %select_n.8), kind=kOutput, calls=%fused_computation.clone.1 | convolution fusion | flops 547356672 | bytes 5392388 | tf_op jit(solution)/shard_map/while/body/eval_jaxpr/dot_general | solution.py:14
  175.9 4.2 %convolution_add_fusion.2 = f32[4096,128]{1,0:T(8,128)S(1)} fusion(bf16[512,4096]{1,0:T(8,128)(2,1)} %add_convert_fusion.2, f32[4096,128]{1,0:T(8,128)S(1)} %get-tuple-element.152, pred[]{:T(512)S(6)} %compare.5, bf16[2048,128]{1,0:T(8,128)(2,1)S(1)} %get-tuple-element.167, s32[]{:T(128)S(6)} %select_n.8), kind=kOutput, calls=%fused_computation.1.clone.1 | convolution fusion | flops 537919488 | bytes 8519685 | tf_op jit(solution)/shard_map/while/body/eval_jaxpr/dot_general | solution.py:56
  180.2 2.0 fusion.22
  182.1 1.4 broadcast_multiply_fusion
  183.7 2.1 bitcast_subtract_fusion
  185.8 3.5 multiply_subtract_fusion
  189.4 82.0 %reduce-scatter.3.cloned.1.call-done = f32[128,128]{1,0:T(8,128)} async-done(((f32[2048,128]{1,0:T(8,128)}), f32[128,128]{1,0:T(8,128)}) %reduce-scatter.3.cloned.1.call-update) | async-done | bytes 65552 | tf_op jit(solution)/shard_map/reduce_scatter | solution.py:70
  271.4 121.0 %reduce-scatter.5.cloned.1.call-done = f32[128,128]{1,0:T(8,128)} async-done(((f32[4096,128]{1,0:T(8,128)}), f32[128,128]{1,0:T(8,128)}) %reduce-scatter.5.cloned.1.call-update) | async-done | bytes 65552 | tf_op jit(solution)/shard_map/reduce_scatter | solution.py:71
  (39 shorter events, 1.9 us)
Async XLA Ops:
  7.2 122.9 %all-gather.4.cloned.1.call-start = ((), (), s32[]{:S(2)}) async-start(), calls=%async_computation.2 | async-start | bytes 1081344 | tf_op jit(solution)/shard_map/all_gather | solution.py:41
  7.9 263.5 %reduce-scatter.3.cloned.1.call-start = ((), (), s32[]{:S(2)}) async-start(), calls=%async_computation.3 | async-start | bytes 1114112 | tf_op jit(solution)/shard_map/reduce_scatter | solution.py:70
  136.9 4.3 %copy-start = (bf16[512,4096]{1,0:T(8,128)(2,1)S(1)}, bf16[512,4096]{1,0:T(8,128)(2,1)}, u32[]{:S(2)}) copy-start(bf16[512,4096]{1,0:T(8,128)(2,1)} %add_convert_fusion.2) | copy-start | bytes 12582916 | tf_op jit(solution)/shard_map/while
  136.9 4.3 %copy-start.1 = (bf16[4096,128]{1,0:T(8,128)(2,1)S(1)}, bf16[4096,128]{1,0:T(8,128)(2,1)}, u32[]{:S(2)}) copy-start(bf16[4096,128]{1,0:T(8,128)(2,1)} %get-tuple-element.168) | copy-start | bytes 3145732 | tf_op jit(solution)/shard_map/while
  149.9 4.3 %copy-start = (bf16[512,4096]{1,0:T(8,128)(2,1)S(1)}, bf16[512,4096]{1,0:T(8,128)(2,1)}, u32[]{:S(2)}) copy-start(bf16[512,4096]{1,0:T(8,128)(2,1)} %add_convert_fusion.2) | copy-start | bytes 12582916 | tf_op jit(solution)/shard_map/while
  149.9 4.3 %copy-start.1 = (bf16[4096,128]{1,0:T(8,128)(2,1)S(1)}, bf16[4096,128]{1,0:T(8,128)(2,1)}, u32[]{:S(2)}) copy-start(bf16[4096,128]{1,0:T(8,128)(2,1)} %get-tuple-element.168) | copy-start | bytes 3145732 | tf_op jit(solution)/shard_map/while
  162.9 4.3 %copy-start = (bf16[512,4096]{1,0:T(8,128)(2,1)S(1)}, bf16[512,4096]{1,0:T(8,128)(2,1)}, u32[]{:S(2)}) copy-start(bf16[512,4096]{1,0:T(8,128)(2,1)} %add_convert_fusion.2) | copy-start | bytes 12582916 | tf_op jit(solution)/shard_map/while
  162.9 4.3 %copy-start.1 = (bf16[4096,128]{1,0:T(8,128)(2,1)S(1)}, bf16[4096,128]{1,0:T(8,128)(2,1)}, u32[]{:S(2)}) copy-start(bf16[4096,128]{1,0:T(8,128)(2,1)} %get-tuple-element.168) | copy-start | bytes 3145732 | tf_op jit(solution)/shard_map/while
  175.9 4.3 %copy-start = (bf16[512,4096]{1,0:T(8,128)(2,1)S(1)}, bf16[512,4096]{1,0:T(8,128)(2,1)}, u32[]{:S(2)}) copy-start(bf16[512,4096]{1,0:T(8,128)(2,1)} %add_convert_fusion.2) | copy-start | bytes 12582916 | tf_op jit(solution)/shard_map/while
  175.9 4.3 %copy-start.1 = (bf16[4096,128]{1,0:T(8,128)(2,1)S(1)}, bf16[4096,128]{1,0:T(8,128)(2,1)}, u32[]{:S(2)}) copy-start(bf16[4096,128]{1,0:T(8,128)(2,1)} %get-tuple-element.168) | copy-start | bytes 3145732 | tf_op jit(solution)/shard_map/while
  182.1 1.5 copy-start.2
  185.8 206.6 %reduce-scatter.5.cloned.1.call-start = ((), (), s32[]{:S(2)}) async-start(), calls=%async_computation.4 | async-start | bytes 2162688 | tf_op jit(solution)/shard_map/reduce_scatter | solution.py:71
Sparse Core Ops, SparseCore 0:
  10.1 72.1 all-gather.3
  185.9 85.4 reduce-scatter.2
  275.0 117.3 reduce-scatter.4
where the time goes:
time: 401 us; the launch traced here: 399 us
  waiting for transfers between devices  204 us (51%)
  blocking collectives  122 us (30%)
  matrix products  46.6 us (12%)
  between operations  13.8 us (3%)
  other arithmetic  7.38 us (2%)
    reduce_scatter x1, waiting for transfers between devices, on_device(): lax.psum_scatter(matched_partner_shard, 'row', scatter_dimension=0, tiled...  121 us
    reduce_scatter x1, waiting for transfers between devices, on_device(): lax.psum_scatter(anchor_local, 'col', scatter_dimension=0, tiled=True)  82 us
    all_gather x1, blocking collectives, on_device(): lax.all_gather(row_lse, 'col', axis=0, tiled=True)  42.7 us
    all_gather x1, blocking collectives, on_device(): lax.all_gather(column_logsumexp, 'row', axis=0, tiled=True)  42.4 us
    all_gather x1, blocking collectives, on_device(): lax.all_gather(anchors, 'col', axis=0, tiled=True)  36.9 us
    dot_general x4, matrix products, soft_weights(): lax.dot_general(anchor_blk, positive_blk, (((1,), (1,)), ((), ())), prefe...  21.8 us
    dot_general x4, matrix products, advance_both(): lax.dot_general(soft, anchor_blk, (((0,), (0,)), ((), ())), preferred_ele...  17 us
  transfers between devices with their start and end apart: 3, of which 2 were waited for; matrix products, arithmetic and copies ran while one was open for 1% of the time, Pallas kernels for 0%

commit v1 on v0

v1 whole, which is shorter than its diff:
```python
import jax
import jax.numpy as jnp
from jax import lax
from jax.experimental import pallas as pl
from jax.experimental.pallas import tpu as pltpu
from jax.sharding import PartitionSpec as P

f32, bf16 = jnp.float32, jnp.bfloat16
MESH = pl.DeviceIdType.MESH
WIDTH = 128
BLOCK = 128
SENT = 144
LOG2E = 1.4426950408889634
SCALE = 10.0 * LOG2E
TOP = 12.0
NUM_Y, NUM_X, NUM_ZH = 8, 4, 4
COLUMNS, ROWS = 32, 16

P_KEYS = [
    (j, dy % NUM_Y, kk) for dy in (0, -1, 1, -2, 2, -3, 3, 4) for j in (0, 1) for kk in (0, 1)
]
A_KEYS = [(dz % NUM_ZH, dx % NUM_X) for dx in (0, -1, 1, 2) for dz in (0, -1, 1, 2)]
P_SLOT = {key: i for i, key in enumerate(P_KEYS)}
A_SLOT = {key: i for i, key in enumerate(A_KEYS)}


def ps(j, dy, kk):
    return P_SLOT[j, dy % NUM_Y, kk]


def as_(dz, dx):
    return A_SLOT[dz % NUM_ZH, dx % NUM_X]


def y_limit(sign, j):
    return 4 if (sign > 0) == (j == 0) else 3


def x_limit(sign, dz):
    return 2 if (sign > 0) == (dz % 2 == 0) else 1


def numbering():
    keys = []
    keys += [("p", i) for i in range(1, COLUMNS)]
    keys += [("a", i) for i in range(1, ROWS)]
    keys += ["pos", "anc"]
    keys += [("core", j, dy) for j in (0, 1) for dy in range(NUM_Y)]
    keys += [
        ("y", s, j, d) for s in (1, -1) for j in (0, 1) for d in range(1, y_limit(s, j) + 1)
    ]
    keys += ["z"]
    keys += [
        ("x", s, dz, d)
        for s in (1, -1)
        for dz in range(NUM_ZH)
        for d in range(1, x_limit(s, dz) + 1)
    ]
    keys += [("zh", 2), ("zh", 1), ("zh", -1)]
    return {key: i for i, key in enumerate(keys)}


SEM = numbering()
SUM_KEYS = [k for k in SEM if k not in ("pos", "anc") and k[0] not in ("p", "a")]
SUM_SLOT = {key: i for i, key in enumerate(SUM_KEYS)}

ROW_TILE, COL_TILE = 4, 16


def kernel(
    a_ref, p_ref, la_ref, lp_ref, da_out, dp_out,
    ab, pb, at, ub, vb, acc_a, acc_p, out_s, in_s, perm, send_sem, recv_sem,
):
    r, c = lax.axis_index("row"), lax.axis_index("col")
    core, y, zl = r % 2, (r // 2) % NUM_Y, r // 16
    x, zh = c % NUM_X, c // NUM_X

    def row_dev(zl_, y_, core_):
        return (zl_ * 16 + y_ * 2 + core_, c)

    def col_dev(zh_, x_):
        return (r, zh_ * NUM_X + x_)

    sibling = row_dev(zl, y, 1 - core)
    z_pair = row_dev(1 - zl, y, core)
    y_dev = {s: row_dev(zl, (y + s + NUM_Y) % NUM_Y, core) for s in (1, -1)}
    x_dev = {s: col_dev(zh, (x + s + NUM_X) % NUM_X) for s in (1, -1)}
    zh_dev = {s: col_dev((zh + s + NUM_ZH) % NUM_ZH, x) for s in (1, -1)}
    q, b = c * COLUMNS + r, r * ROWS + c
    pos_dev = (q // ROWS, q % ROWS)
    anc_dev = (b % COLUMNS, b // COLUMNS)
    moves = q != b

    peers = [sibling, z_pair, *y_dev.values(), *x_dev.values(), *zh_dev.values()]
    barrier = pltpu.get_barrier_semaphore()
    for dev in peers:
        pl.semaphore_signal(barrier, inc=1, device_id=dev, device_id_type=MESH)

    @pl.when(moves)
    def _():
        for dev in (pos_dev, anc_dev):
            pl.semaphore_signal(barrier, inc=1, device_id=dev, device_id_type=MESH)

    ab[0, :BLOCK, :] = a_ref[...]
    pb[0, :BLOCK, :] = p_ref[...]
    ab[0, BLOCK:, :] = jnp.broadcast_to(la_ref[...], (SENT - BLOCK, WIDTH))
    pb[0, BLOCK:, :] = jnp.broadcast_to(lp_ref[...], (SENT - BLOCK, WIDTH))

    pl.semaphore_wait(barrier, len(peers) + 2 * moves.astype(jnp.int32))

    copies = {}

    def send(key, src, dst, dev):
        copy = pltpu.make_async_remote_copy(
            src_ref=src, dst_ref=dst, send_sem=send_sem.at[SEM[key]], recv_sem=recv_sem.at[SEM[key]],
            device_id=dev, device_id_type=MESH,
        )
        copy.start()
        copies[key] = copy

    def send_p(src, dst, dev):
        send(("p", dst), pb.at[src], pb.at[dst], dev)

    def send_a(src, dst, dev):
        send(("a", dst), ab.at[src], ab.at[dst], dev)

    def got(key):
        copies[key].wait_recv()

    def perm_copies():
        return [
            pltpu.make_async_remote_copy(
                src_ref=src, dst_ref=perm.at[i], send_sem=send_sem.at[SEM[key]],
                recv_sem=recv_sem.at[SEM[key]], device_id=dev, device_id_type=MESH,
            )
            for i, (key, src, dev) in enumerate(
                [("pos", pb.at[0, pl.ds(0, BLOCK)], pos_dev), ("anc", ab.at[0, pl.ds(0, BLOCK)], anc_dev)]
            )
        ]

    send_a(as_(0, 0), as_(-1, 0), zh_dev[1])
    send_a(as_(0, 0), as_(1, 0), zh_dev[-1])
    send_p(ps(0, 0, 0), ps(1, 0, 0), z_pair)
    for s in (1, -1):
        send_p(ps(0, 0, 0), ps(0, -s, 0), y_dev[s])
        send_a(as_(0, 0), as_(0, -s), x_dev[s])
    send_p(ps(0, 0, 0), ps(0, 0, 1), sibling)

    def on_a_z(dz):
        got(("a", as_(dz, 0)))
        if dz == -1:
            send_a(as_(-1, 0), as_(2, 0), zh_dev[1])
        for s in (1, -1):
            send_a(as_(dz, 0), as_(dz, -s), x_dev[s])

    def on_a_x(dz, s):
        got(("a", as_(dz, -s)))
        if x_limit(s, dz) == 2:
            send_a(as_(dz, -s), as_(dz, 2), x_dev[s])

    def on_p_z():
        got(("p", ps(1, 0, 0)))
        for s in (1, -1):
            send_p(ps(1, 0, 0), ps(1, -s, 0), y_dev[s])
        send_p(ps(1, 0, 0), ps(1, 0, 1), sibling)

    def on_p_y(j, s, d):
        got(("p", ps(j, -s * d, 0)))
        if d < y_limit(s, j):
            send_p(ps(j, -s * d, 0), ps(j, -s * (d + 1), 0), y_dev[s])
        send_p(ps(j, -s * d, 0), ps(j, -s * d, 1), sibling)

    on_p_z()
    on_a_z(-1)
    on_a_z(1)
    for s in (1, -1):
        on_p_y(0, s, 1)
        on_a_x(0, s)
    for s in (1, -1):
        on_p_y(1, s, 1)
    on_a_z(2)

    @pl.when(moves)
    def _():
        for copy in perm_copies():
            copy.start()

    for s in (1, -1):
        on_a_x(-1, s)
        on_a_x(1, s)
    for s in (1, -1):
        on_p_y(0, s, 2)
        on_p_y(1, s, 2)
    for s in (1, -1):
        on_a_x(2, s)
    for s in (1, -1):
        on_p_y(0, s, 3)
        on_p_y(1, s, 3)
    for dz in range(NUM_ZH):
        got(("a", as_(dz, 2)))
    on_p_y(0, 1, 4)
    on_p_y(1, -1, 4)
    for j, dy, kk in P_KEYS:
        if kk:
            got(("p", ps(j, dy, 1)))

    def prepare_a(i, _):
        block = ab[i, :BLOCK, :].astype(f32)
        rows = pl.ds(pl.multiple_of(i * BLOCK, BLOCK), BLOCK)
        at[:, rows] = block.T.astype(bf16)
        lse = ab[i, BLOCK:, :].astype(f32)[0:1, :]
        ub[rows, :] = jnp.broadcast_to(jnp.exp(TOP - lse), (BLOCK, BLOCK)).T
        return 0

    def prepare_p(i, _):
        lse = pb[i, BLOCK:, :].astype(f32)[0:8, :]
        vb[:, pl.ds(pl.multiple_of(i * BLOCK, BLOCK), BLOCK)] = jnp.exp(TOP - lse)
        return 0

    lax.fori_loop(0, ROWS, prepare_a, 0)
    lax.fori_loop(0, COLUMNS, prepare_p, 0)
    acc_a[...] = jnp.zeros_like(acc_a)
    acc_p[...] = jnp.zeros_like(acc_p)

    rt, ct = ROW_TILE * BLOCK, COL_TILE * BLOCK

    def tile(n, _):
        i, j = n // (COLUMNS // COL_TILE), n % (COLUMNS // COL_TILE)
        rows, cols = pl.ds(pl.multiple_of(i * rt, rt), rt), pl.ds(pl.multiple_of(j * ct, ct), ct)
        a = ab[pl.ds(i * ROW_TILE, ROW_TILE), :BLOCK, :].reshape(rt, WIDTH)
        p = pb[pl.ds(j * COL_TILE, COL_TILE), :BLOCK, :].reshape(ct, WIDTH)
        t = lax.dot_general(a, p, (((1,), (1,)), ((), ())), preferred_element_type=f32)
        weight = jnp.concatenate([ub[rows, :]] * COL_TILE, axis=1) + vb[0:1, cols]
        soft = (jnp.exp2(t * SCALE - TOP * LOG2E) * weight).astype(bf16)
        acc_a[rows, :] += jnp.dot(soft, p, preferred_element_type=f32)
        acc_p[:, cols] += jnp.dot(at[:, rows], soft, preferred_element_type=f32)
        return 0

    lax.fori_loop(0, (ROWS // ROW_TILE) * (COLUMNS // COL_TILE), tile, 0)

    def own_a(dz, dx):
        i = as_(dz, dx)
        return acc_a[i * BLOCK:(i + 1) * BLOCK, :]

    def own_p(j, dy, kk):
        i = ps(j, dy, kk)
        return acc_p[:, i * BLOCK:(i + 1) * BLOCK]

    def send_sum(key, value, dev):
        i = SUM_SLOT[key]
        out_s[i] = value.astype(bf16)
        send(key, out_s.at[i], in_s.at[i], dev)

    def arrived(key):
        got(key)
        return in_s[SUM_SLOT[key]].astype(f32)

    def chip_p(j, dy):
        return own_p(j, dy, 0) + arrived(("core", j, dy % NUM_Y))

    def y_step(s, j, d):
        value = chip_p(j, s * d)
        if d < y_limit(s, j):
            value += arrived(("y", s, j, d + 1))
        send_sum(("y", s, j, d), value, y_dev[s])

    def x_step(s, dz, d):
        value = own_a(dz, s * d)
        if d < x_limit(s, dz):
            value += arrived(("x", s, dz, d + 1))
        send_sum(("x", s, dz, d), value, x_dev[s])

    def x_total(dz):
        return own_a(dz, 0) + arrived(("x", 1, dz, 1)) + arrived(("x", -1, dz, 1))

    for dy in (4, 3, -3, 2, -2, 1, -1, 0):
        for j in (0, 1):
            send_sum(("core", j, dy % NUM_Y), own_p(j, dy, 1), sibling)
    x_step(1, 2, 2)
    x_step(-1, 1, 2)
    x_step(1, 0, 2)
    x_step(-1, 3, 2)
    y_step(1, 0, 4)
    y_step(-1, 1, 4)
    y_step(1, 1, 3)
    y_step(-1, 0, 3)
    for s in (1, -1):
        for dz in (2, 1, 3, 0):
            if x_limit(s, dz) == 1:
                x_step(s, dz, 1)
    y_step(1, 0, 3)
    y_step(-1, 1, 3)
    x_step(1, 2, 1)
    x_step(-1, 1, 1)
    x_step(1, 0, 1)
    x_step(-1, 3, 1)
    for d in (2, 1):
        y_step(1, 1, d)
        y_step(-1, 0, d)
        y_step(1, 0, d)
        y_step(-1, 1, d)
        if d == 2:
            send_sum(("zh", 2), x_total(2), zh_dev[1])
            send_sum(("zh", -1), x_total(-1 % NUM_ZH), zh_dev[-1])
            send_sum(("zh", 1), x_total(1) + arrived(("zh", 2)), zh_dev[1])

    def y_total(j):
        return chip_p(j, 0) + arrived(("y", 1, j, 1)) + arrived(("y", -1, j, 1))

    send_sum("z", y_total(1), z_pair)

    @pl.when(moves)
    def _():
        for copy in perm_copies():
            copy.wait()

    @pl.when(jnp.logical_not(moves))
    def _():
        perm[0] = pb[0, :BLOCK, :]
        perm[1] = ab[0, :BLOCK, :]

    total_a = x_total(0) + arrived(("zh", 1)) + arrived(("zh", -1))
    da_out[...] = 5.0 * total_a - 10.0 * perm[0].astype(f32)
    total_p = y_total(0) + arrived("z")
    dp_out[...] = 5.0 * total_p.T - 10.0 * perm[1].astype(f32)
    for copy in copies.values():
        copy.wait_send()


def on_device(anchors, positives, row_lse, column_logsumexp):
    vmem = pl.BlockSpec(memory_space=pltpu.VMEM)
    block = jax.ShapeDtypeStruct((BLOCK, WIDTH), f32)
    return pl.pallas_call(
        kernel,
        out_shape=(block, block),
        in_specs=[vmem] * 4,
        out_specs=(vmem, vmem),
        scratch_shapes=[
            pltpu.VMEM((ROWS, SENT, WIDTH), bf16),
            pltpu.VMEM((COLUMNS, SENT, WIDTH), bf16),
            pltpu.VMEM((WIDTH, ROWS * BLOCK), bf16),
            pltpu.VMEM((ROWS * BLOCK, BLOCK), f32),
            pltpu.VMEM((8, COLUMNS * BLOCK), f32),
            pltpu.VMEM((ROWS * BLOCK, WIDTH), f32),
            pltpu.VMEM((WIDTH, COLUMNS * BLOCK), f32),
            pltpu.VMEM((len(SUM_KEYS), BLOCK, WIDTH), bf16),
            pltpu.VMEM((len(SUM_KEYS), BLOCK, WIDTH), bf16),
            pltpu.VMEM((2, BLOCK, WIDTH), bf16),
            pltpu.SemaphoreType.DMA((len(SEM),)),
            pltpu.SemaphoreType.DMA((len(SEM),)),
        ],
        compiler_params=pltpu.CompilerParams(
            collective_id=0, has_side_effects=True, vmem_limit_bytes=48 * 2**20
        ),
        name="infonce_backward",
    )(anchors, positives, row_lse.reshape(1, BLOCK), column_logsumexp.reshape(1, BLOCK))


def solution(mesh):
    return jax.shard_map(
        on_device,
        mesh=mesh,
        in_specs=(
            P(("row", "col"), None),
            P(("col", "row"), None),
            P(("row", "col")),
            P(("col", "row")),
        ),
        out_specs=(P(("row", "col"), None), P(("col", "row"), None)),
        check_vma=False,
    )
```

time: 401 us -> 75.1 us (0.19)
  waiting for transfers between devices: 204 us -> 0 us
  blocking collectives: 122 us -> 0 us
  Pallas kernels: 0 us -> 69.6 us
  matrix products: 46.6 us -> 0 us
  between operations: 13.8 us -> 0.66 us
  other arithmetic: 7.38 us -> 0 us
    reduce_scatter x2 -> x0, waiting for transfers between devices: 203 us -> none  [the longest x1 121 us: on_device(): lax.psum_scatter(matched_partner_shard, 'row', scatter_dimension=0, tiled...]
    all_gather x3 -> x0, blocking collectives: 122 us -> none  [the longest x1 42.7 us: on_device(): lax.all_gather(row_lse, 'col', axis=0, tiled=True)]
    pallas_call x0 -> x1, Pallas kernels: none -> 69.6 us  [on_device(): pl.pallas_call(kernel, out_shape=(block, block), in_specs=[vmem] * 4, out...]
    dot_general x12 -> x0, matrix products: 46.6 us -> none  [the longest x4 21.8 us: soft_weights(): lax.dot_general(anchor_blk, positive_blk, (((1,), (1,)), ((), ())), prefe...]
    sub x2 -> x0, other arithmetic: 5.59 us -> none  [the longest x1 3.51 us: on_device(): half_inverse * positive_summed]
  transfers between devices with their start and end apart: 3 -> 0, of which waited for: 2 -> 0; matrix products, arithmetic and copies ran while one was open for 1% -> 0% of each run, Pallas kernels for 0% -> 0%
where the time goes in v1:
time: 75.1 us; the launch traced here: 73.7 us
  Pallas kernels  69.6 us (93%)
  local copies, waits for them, and re-layouts  3.43 us (5%)
    pallas_call x1, Pallas kernels, on_device(): pl.pallas_call(kernel, out_shape=(block, block), in_specs=[vmem] * 4, out...  69.6 us
    unnamed x10, local copies, waits for them, and re-layouts  3.43 us

profile of v1, /device:TPU:1, one launch (start us, length us, event | category | flops | bytes accessed | tf_op | source)
XLA Modules:
  0.0 73.7 jit_solution(403432835556485276)
XLA Ops:
  0.6 0.0 copy-start.2
  0.6 0.0 copy-start.3
  0.7 0.6 copy-done.2
  1.3 0.0 copy-done.3
  1.3 0.0 copy-start
  1.3 0.8 %copy-done = bf16[128,128]{1,0:T(8,128)(2,1)S(1)} copy-done((bf16[128,128]{1,0:T(8,128)(2,1)S(1)}, bf16[128,128]{1,0:T(8,128)(2,1)}, u32[]{:S(2)}) %copy-start) | copy-done | bytes 32792
  2.1 0.0 copy-start.1
  2.1 0.8 %copy-done.1 = bf16[128,128]{1,0:T(8,128)(2,1)S(1)} copy-done((bf16[128,128]{1,0:T(8,128)(2,1)S(1)}, bf16[128,128]{1,0:T(8,128)(2,1)}, u32[]{:S(2)}) %copy-start.1) | copy-done | bytes 32792
  2.8 69.6 %infonce_backward.1 = (f32[128,128]{1,0:T(8,128)S(1)}, f32[128,128]{1,0:T(8,128)S(1)}) custom-call(bf16[128,128]{1,0:T(8,128)(2,1)S(1)} %copy-done, bf16[128,128]{1,0:T(8,128)(2,1)S(1)} %copy-done.1, bf16[1,128]{1,0:T(2,128)(2,1)S(1)} %bitcast.2, bf16[1,128]{1,0:T(2,128)(2,1)S(1)} %bitcast.3), custom_call_target="tpu_custom_call" | custom-call | tf_op jit(solution)/shard_map/infonce_backward/pallas_call | solution.py:333
  72.4 0.6 copy.8
  73.0 0.6 copy.9
Async XLA Ops:
  0.6 0.7 copy-start.2
  0.6 0.7 copy-start.3
  1.3 0.8 %copy-start = (bf16[128,128]{1,0:T(8,128)(2,1)S(1)}, bf16[128,128]{1,0:T(8,128)(2,1)}, u32[]{:S(2)}) copy-start(bf16[128,128]{1,0:T(8,128)(2,1)} %a_ref.1) | copy-start | bytes 98308
  2.1 0.8 %copy-start.1 = (bf16[128,128]{1,0:T(8,128)(2,1)S(1)}, bf16[128,128]{1,0:T(8,128)(2,1)}, u32[]{:S(2)}) copy-start(bf16[128,128]{1,0:T(8,128)(2,1)} %p_ref.1) | copy-start | bytes 98308

commit v2 on v0

v2 whole, which is shorter than its diff:
```python
import jax
import jax.numpy as jnp
from jax import lax
from jax.experimental import pallas as pl
from jax.experimental.pallas import tpu as pltpu
from jax.sharding import PartitionSpec as P

f32, bf16 = jnp.float32, jnp.bfloat16
MESH = pl.DeviceIdType.MESH
WIDTH = 128
BLOCK = 128
SENT = 144
LOG2E = 1.4426950408889634
SCALE = 10.0 * LOG2E
TOP = 12.0
NUM_Y, NUM_X, NUM_ZH = 8, 4, 4
COLUMNS, ROWS = 32, 16

P_GROUPS = {
    "home": [(0, 0), (1, 0)],
    "near": [(0, -1), (0, 1)],
    "next": [(0, -2), (0, 2)],
    "pair_near": [(1, -1), (1, 1)],
    "far": [(0, -3), (0, 3), (0, 4)],
    "pair_next": [(1, -2), (1, 2)],
    "pair_far": [(1, -3), (1, 3), (1, 4)],
}
P_KEYS = [(j, dy % NUM_Y, kk) for group in P_GROUPS.values() for j, dy in group for kk in (0, 1)]
A_KEYS = [(dz % NUM_ZH, dx % NUM_X) for dz in (0, -1, 1, 2) for dx in (0, -1, 1, 2)]
P_SLOT = {key: i for i, key in enumerate(P_KEYS)}
A_SLOT = {key: i for i, key in enumerate(A_KEYS)}


def ps(j, dy, kk):
    return P_SLOT[j, dy % NUM_Y, kk]


def as_(dz, dx):
    return A_SLOT[dz % NUM_ZH, dx % NUM_X]


def p_slots(*names):
    slots = [ps(j, dy, kk) for name in names for j, dy in P_GROUPS[name] for kk in (0, 1)]
    assert slots == list(range(slots[0], slots[0] + len(slots)))
    return slots[0], len(slots)


def a_slots(*dzs):
    slots = [as_(dz, dx) for dz in dzs for dx in (0, -1, 1, 2)]
    assert slots == list(range(slots[0], slots[0] + len(slots)))
    return slots[0], len(slots)


def numbering():
    keys = []
    keys += [("p", i) for i in range(1, COLUMNS)]
    keys += [("a", i) for i in range(1, ROWS)]
    keys += [("core", j, dy) for j in (0, 1) for dy in range(NUM_Y)]
    keys += [("y", j, dy) for j in (0, 1) for dy in range(1, NUM_Y)]
    keys += [("z",)]
    keys += [("x", dz, dx) for dz in range(NUM_ZH) for dx in range(1, NUM_X)]
    keys += [("zh", dz) for dz in range(1, NUM_ZH)]
    return {key: i for i, key in enumerate(keys)}


SEM = numbering()
SUM_KEYS = [k for k in SEM if k[0] not in ("p", "a")]
SUM_SLOT = {key: i for i, key in enumerate(SUM_KEYS)}

BARRIER_Y, BARRIER_ZH = (1, 2, 6, 7), (1, 3)


def kernel(
    a_ref, p_ref, la_ref, lp_ref, da_out, dp_out,
    ab, pb, at, ub, vb, acc_a, acc_p, out_s, in_s, send_sem, recv_sem, load_sem,
):
    loads = [
        pltpu.make_async_copy(a_ref, ab.at[0, pl.ds(0, BLOCK)], load_sem.at[0]),
        pltpu.make_async_copy(p_ref, pb.at[0, pl.ds(0, BLOCK)], load_sem.at[1]),
    ]
    for load in loads:
        load.start()

    r, c = lax.axis_index("row"), lax.axis_index("col")
    core, y, zl = r % 2, (r // 2) % NUM_Y, r // 16
    x, zh = c % NUM_X, c // NUM_X

    def row_dev(zl_, y_, core_):
        return (zl_ * 16 + y_ * 2 + core_, c)

    def col_dev(zh_, x_):
        return (r, zh_ * NUM_X + x_)

    sibling = row_dev(zl, y, 1 - core)
    z_pair = row_dev(1 - zl, y, core)
    y_dev = {d: row_dev(zl, (y + d) % NUM_Y, core) for d in range(1, NUM_Y)}
    x_dev = {d: col_dev(zh, (x + d) % NUM_X) for d in range(1, NUM_X)}
    zh_dev = {d: col_dev((zh + d) % NUM_ZH, x) for d in range(1, NUM_ZH)}

    peers = [sibling, z_pair, *x_dev.values()]
    peers += [y_dev[d] for d in BARRIER_Y] + [zh_dev[d] for d in BARRIER_ZH]
    barrier = pltpu.get_barrier_semaphore()
    for dev in peers:
        pl.semaphore_signal(barrier, inc=1, device_id=dev, device_id_type=MESH)
    ab[0, BLOCK:, :] = jnp.broadcast_to(la_ref[...], (SENT - BLOCK, WIDTH))
    pb[0, BLOCK:, :] = jnp.broadcast_to(lp_ref[...], (SENT - BLOCK, WIDTH))
    for load in loads:
        load.wait()
    pl.semaphore_wait(barrier, len(peers))

    copies = {}

    def send(key, src, dst, dev):
        copy = pltpu.make_async_remote_copy(
            src_ref=src, dst_ref=dst, send_sem=send_sem.at[SEM[key]], recv_sem=recv_sem.at[SEM[key]],
            device_id=dev, device_id_type=MESH,
        )
        copy.start()
        copies[key] = copy

    def got(key):
        copies[key].wait_recv()

    def send_p(src, dst, dev):
        send(("p", dst), pb.at[src], pb.at[dst], dev)

    def send_a(src, dst, dev):
        send(("a", dst), ab.at[src], ab.at[dst], dev)

    def got_p(j, dy, kk):
        got(("p", ps(j, dy, kk)))

    def got_a(dz, dx):
        got(("a", as_(dz, dx)))

    def a_along_x(dz):
        for d in (1, -1, 2):
            send_a(as_(dz, 0), as_(dz, -d), x_dev[d % NUM_X])

    def p_along_y(j, ds):
        for d in ds:
            send_p(ps(j, 0, 0), ps(j, -d, 0), y_dev[d % NUM_Y])

    def to_sibling(j, dy):
        send_p(ps(j, dy, 0), ps(j, dy, 1), sibling)

    def onward(j, s):
        got_p(j, -2 * s, 0)
        send_p(ps(j, -2 * s, 0), ps(j, -3 * s, 0), y_dev[s % NUM_Y])
        if (s > 0) == (j == 0):
            send_p(ps(j, -2 * s, 0), ps(j, 4, 0), y_dev[2 * s % NUM_Y])
        to_sibling(j, -2 * s)

    def prepare_a(dz):
        first, count = a_slots(dz)
        for i in range(first, first + count):
            rows = slice(i * BLOCK, (i + 1) * BLOCK)
            at[:, rows] = ab[i, :BLOCK, :].astype(f32).T.astype(bf16)
            lse = ab[i, BLOCK:, :].astype(f32)[0:1, :]
            ub[rows, :] = jnp.broadcast_to(jnp.exp(TOP - lse), (BLOCK, BLOCK)).T

    def prepare_p(name):
        first, count = p_slots(name)
        for i in range(first, first + count):
            lse = pb[i, BLOCK:, :].astype(f32)[0:8, :]
            vb[:, i * BLOCK:(i + 1) * BLOCK] = jnp.exp(TOP - lse)

    touched = set()

    def tile(row_slots, col_slots):
        (r0, nr), (c0, nc) = row_slots, col_slots
        rows, cols = slice(r0 * BLOCK, (r0 + nr) * BLOCK), slice(c0 * BLOCK, (c0 + nc) * BLOCK)
        a = ab[r0:r0 + nr, :BLOCK, :].reshape(nr * BLOCK, WIDTH)
        p = pb[c0:c0 + nc, :BLOCK, :].reshape(nc * BLOCK, WIDTH)
        t = lax.dot_general(a, p, (((1,), (1,)), ((), ())), preferred_element_type=f32)
        weight = jnp.concatenate([ub[rows, :]] * nc, axis=1) + vb[0:1, cols]
        soft = (jnp.exp2(t * SCALE - TOP * LOG2E) * weight).astype(bf16)
        to_rows = jnp.dot(soft, p, preferred_element_type=f32)
        to_cols = jnp.dot(at[:, rows], soft, preferred_element_type=f32)
        row_keys = {("a", i) for i in range(r0, r0 + nr)}
        col_keys = {("p", i) for i in range(c0, c0 + nc)}
        if row_keys <= touched:
            acc_a[rows, :] += to_rows
        else:
            assert not row_keys & touched
            acc_a[rows, :] = to_rows
        if col_keys <= touched:
            acc_p[:, cols] += to_cols
        else:
            assert not col_keys & touched
            acc_p[:, cols] = to_cols
        touched.update(row_keys | col_keys)

    def own_a(dz, dx):
        i = as_(dz, dx)
        return acc_a[i * BLOCK:(i + 1) * BLOCK, :]

    def own_p(j, dy, kk):
        i = ps(j, dy, kk)
        return acc_p[:, i * BLOCK:(i + 1) * BLOCK]

    def send_sum(key, value, dev):
        i = SUM_SLOT[key]
        out_s[i] = value.astype(bf16)
        send(key, out_s.at[i], in_s.at[i], dev)

    def arrived(*key):
        got(key)
        return in_s[SUM_SLOT[key]].astype(f32)

    def core_sums(*names):
        for name in names:
            for j, dy in P_GROUPS[name]:
                send_sum(("core", j, dy % NUM_Y), own_p(j, dy, 1), sibling)

    def chip_sum(j, dy):
        return own_p(j, dy, 0) + arrived("core", j, dy % NUM_Y)

    def y_sums(*names):
        for name in names:
            for j, dy in P_GROUPS[name]:
                send_sum(("y", j, dy % NUM_Y), chip_sum(j, dy), y_dev[dy % NUM_Y])

    def y_total(j):
        total = chip_sum(j, 0)
        for dy in range(1, NUM_Y):
            total += arrived("y", j, dy)
        return total

    def x_sums(dz):
        for dx in (2, 1, -1):
            send_sum(("x", dz % NUM_ZH, dx % NUM_X), own_a(dz, dx), x_dev[dx % NUM_X])

    def x_total(dz):
        total = own_a(dz, 0)
        for dx in range(1, NUM_X):
            total += arrived("x", dz % NUM_ZH, dx)
        return total

    def zh_sum(dz):
        send_sum(("zh", dz % NUM_ZH), x_total(dz), zh_dev[dz % NUM_ZH])

    def diagonal():
        for dz, dx in A_KEYS:
            i = as_(dz, dx)
            other = (zh + dz) % NUM_ZH * NUM_X + (x + dx) % NUM_X
            j, dy, kk = (core + zl) % 2, (other // 2 + NUM_Y - y) % NUM_Y, (other + core) % 2
            place = jnp.where(dy <= 3, 2 * dy, 15 - 2 * dy)
            k = jnp.where(
                place == 0, 2 * j,
                jnp.where(
                    place <= 2, 4 + 8 * j + 2 * (place - 1),
                    jnp.where(place <= 4, 8 + 14 * j + 2 * (place - 3), 16 + 10 * j + 2 * (place - 5)),
                ),
            ) + kk
            rows, cols = slice(i * BLOCK, (i + 1) * BLOCK), pl.ds(pl.multiple_of(k * BLOCK, BLOCK), BLOCK)
            acc_a[rows, :] -= 2.0 * pb[k, :BLOCK, :].astype(f32)
            acc_p[:, cols] -= 2.0 * at[:, rows].astype(f32)

    send_a(as_(0, 0), as_(-1, 0), zh_dev[1])
    send_a(as_(0, 0), as_(1, 0), zh_dev[3])
    send_p(ps(0, 0, 0), ps(1, 0, 0), z_pair)
    p_along_y(0, (1, -1))
    a_along_x(0)
    p_along_y(0, (2, -2))
    to_sibling(0, 0)

    got_p(1, 0, 0)
    p_along_y(1, (1, -1, 2, -2))
    to_sibling(1, 0)
    for s in (1, -1):
        got_p(0, s, 0)
        to_sibling(0, s)
    got_a(-1, 0)
    send_a(as_(-1, 0), as_(2, 0), zh_dev[1])
    a_along_x(-1)
    got_a(1, 0)
    a_along_x(1)
    for d in (1, -1, 2):
        got_a(0, d)
    prepare_a(0)
    for s in (1, -1):
        got_p(0, s, 1)
    prepare_p("near")
    tile(a_slots(0), p_slots("near"))

    onward(0, 1)
    onward(0, -1)
    for s in (1, -1):
        got_p(0, 2 * s, 1)
    prepare_p("next")
    tile(a_slots(0), p_slots("next"))

    for s in (1, -1):
        got_p(1, s, 0)
        to_sibling(1, s)
    got_a(2, 0)
    a_along_x(2)
    for dz in (-1, 1):
        for d in (1, -1, 2):
            got_a(dz, d)
        prepare_a(dz)
        tile(a_slots(dz), p_slots("near", "next"))
        if dz == -1:
            onward(1, 1)
            onward(1, -1)
            for d in (3, -3, 4):
                got_p(0, d, 0)
                to_sibling(0, d)
    for s in (1, -1):
        got_p(1, s, 1)
    prepare_p("pair_near")
    tile(a_slots(0, -1, 1), p_slots("pair_near"))

    for d in (1, -1, 2):
        got_a(2, d)
    prepare_a(2)
    tile(a_slots(2), p_slots("near", "next", "pair_near"))

    for d in (3, -3, 4):
        got_p(1, d, 0)
        to_sibling(1, d)
    for d in (3, -3, 4):
        got_p(0, d, 1)
    prepare_p("far")
    for d in (2, -2):
        got_p(1, d, 1)
    prepare_p("pair_next")
    for d in (3, -3, 4):
        got_p(1, d, 1)
    prepare_p("pair_far")
    got_p(0, 0, 1)
    got_p(1, 0, 1)
    prepare_p("home")
    tile(a_slots(2), p_slots("home"))
    tile(a_slots(2), p_slots("far", "pair_next", "pair_far"))

    @pl.when(c == r // 2)
    def _():
        diagonal()

    core_sums("near", "next", "pair_near")
    x_sums(2)
    others = a_slots(0, -1, 1)
    tile(others, p_slots("far"))
    core_sums("far")
    y_sums("near", "next", "pair_near")
    tile(others, p_slots("pair_far"))
    core_sums("pair_far")
    y_sums("far")
    zh_sum(2)
    tile(others, p_slots("pair_next"))
    core_sums("pair_next")
    y_sums("pair_far")
    tile(a_slots(-1), p_slots("home"))
    x_sums(-1)
    y_sums("pair_next")
    tile(a_slots(1), p_slots("home"))
    x_sums(1)
    tile(a_slots(0), p_slots("home"))
    core_sums("home")
    x_sums(0)
    zh_sum(-1)
    zh_sum(1)
    send_sum(("z",), y_total(1), z_pair)
    total_a = x_total(0)
    for dz in (2, 1, 3):
        total_a += arrived("zh", dz)
    da_out[...] = 5.0 * total_a
    total_p = y_total(0) + arrived("z")
    dp_out[...] = 5.0 * total_p.T
    for copy in copies.values():
        copy.wait_send()


def on_device(anchors, positives, row_lse, column_logsumexp):
    vmem = pl.BlockSpec(memory_space=pltpu.VMEM)
    anywhere = pl.BlockSpec(memory_space=pl.ANY)
    block = jax.ShapeDtypeStruct((BLOCK, WIDTH), f32)
    return pl.pallas_call(
        kernel,
        out_shape=(block, block),
        in_specs=[anywhere, anywhere, vmem, vmem],
        out_specs=(vmem, vmem),
        scratch_shapes=[
            pltpu.VMEM((ROWS, SENT, WIDTH), bf16),
            pltpu.VMEM((COLUMNS, SENT, WIDTH), bf16),
            pltpu.VMEM((WIDTH, ROWS * BLOCK), bf16),
            pltpu.VMEM((ROWS * BLOCK, BLOCK), f32),
            pltpu.VMEM((8, COLUMNS * BLOCK), f32),
            pltpu.VMEM((ROWS * BLOCK, WIDTH), f32),
            pltpu.VMEM((WIDTH, COLUMNS * BLOCK), f32),
            pltpu.VMEM((len(SUM_KEYS), BLOCK, WIDTH), bf16),
            pltpu.VMEM((len(SUM_KEYS), BLOCK, WIDTH), bf16),
            pltpu.SemaphoreType.DMA((len(SEM),)),
            pltpu.SemaphoreType.DMA((len(SEM),)),
            pltpu.SemaphoreType.DMA((2,)),
        ],
        compiler_params=pltpu.CompilerParams(
            collective_id=0, has_side_effects=True, vmem_limit_bytes=48 * 2**20
        ),
        name="infonce_backward",
    )(anchors, positives, row_lse.reshape(1, BLOCK), column_logsumexp.reshape(1, BLOCK))


def solution(mesh):
    return jax.shard_map(
        on_device,
        mesh=mesh,
        in_specs=(
            P(("row", "col"), None),
            P(("col", "row"), None),
            P(("row", "col")),
            P(("col", "row")),
        ),
        out_specs=(P(("row", "col"), None), P(("col", "row"), None)),
        check_vma=False,
    )
```

time: 401 us -> 57.7 us (0.14)
  waiting for transfers between devices: 204 us -> 0 us
  blocking collectives: 122 us -> 0 us
  Pallas kernels: 0 us -> 53.4 us
  matrix products: 46.6 us -> 0 us
  between operations: 13.8 us -> 0.66 us
  other arithmetic: 7.38 us -> 0 us
    reduce_scatter x2 -> x0, waiting for transfers between devices: 203 us -> none  [the longest x1 121 us: on_device(): lax.psum_scatter(matched_partner_shard, 'row', scatter_dimension=0, tiled...]
    all_gather x3 -> x0, blocking collectives: 122 us -> none  [the longest x1 42.7 us: on_device(): lax.all_gather(row_lse, 'col', axis=0, tiled=True)]
    pallas_call x0 -> x1, Pallas kernels: none -> 53.4 us  [on_device(): pl.pallas_call(kernel, out_shape=(block, block), in_specs=[anywhere, anyw...]
    dot_general x12 -> x0, matrix products: 46.6 us -> none  [the longest x4 21.8 us: soft_weights(): lax.dot_general(anchor_blk, positive_blk, (((1,), (1,)), ((), ())), prefe...]
    sub x2 -> x0, other arithmetic: 5.59 us -> none  [the longest x1 3.51 us: on_device(): half_inverse * positive_summed]
  transfers between devices with their start and end apart: 3 -> 0, of which waited for: 2 -> 0; matrix products, arithmetic and copies ran while one was open for 1% -> 0% of each run, Pallas kernels for 0% -> 0%
where the time goes in v2:
time: 57.7 us; the launch traced here: 57.4 us
  Pallas kernels  53.4 us (93%)
  local copies, waits for them, and re-layouts  3.43 us (6%)
  between operations  0.66 us (1%)
    pallas_call x1, Pallas kernels, on_device(): pl.pallas_call(kernel, out_shape=(block, block), in_specs=[anywhere, anyw...  53.4 us
    unnamed x10, local copies, waits for them, and re-layouts  3.43 us

profile of v2, /device:TPU:1, one launch (start us, length us, event | category | flops | bytes accessed | tf_op | source)
XLA Modules:
  0.0 57.4 jit_solution(9302583648399415568)
XLA Ops:
  0.6 0.0 copy-start.2
  0.6 0.0 copy-start.3
  0.7 0.6 %copy-done.2 = bf16[128]{0:T(256)(128)(2,1)S(1)} copy-done((bf16[128]{0:T(256)(128)(2,1)S(1)}, bf16[128]{0:T(256)(128)(2,1)}, u32[]{:S(2)}) %copy-start.2) | copy-done | bytes 280
  1.3 0.0 copy-done.3
  1.3 0.0 copy-start
  1.3 0.8 %copy-done = bf16[128,128]{1,0:T(8,128)(2,1)S(1)} copy-done((bf16[128,128]{1,0:T(8,128)(2,1)S(1)}, bf16[128,128]{1,0:T(8,128)(2,1)}, u32[]{:S(2)}) %copy-start) | copy-done | bytes 32792
  2.1 0.0 copy-start.1
  2.1 0.8 %copy-done.1 = bf16[128,128]{1,0:T(8,128)(2,1)S(1)} copy-done((bf16[128,128]{1,0:T(8,128)(2,1)S(1)}, bf16[128,128]{1,0:T(8,128)(2,1)}, u32[]{:S(2)}) %copy-start.1) | copy-done | bytes 32792
  2.8 53.4 %infonce_backward.1 = (f32[128,128]{1,0:T(8,128)S(1)}, f32[128,128]{1,0:T(8,128)S(1)}) custom-call(bf16[128,128]{1,0:T(8,128)(2,1)S(1)} %copy-done, bf16[128,128]{1,0:T(8,128)(2,1)S(1)} %copy-done.1, bf16[1,128]{1,0:T(2,128)(2,1)S(1)} %bitcast.2, bf16[1,128]{1,0:T(2,128)(2,1)S(1)} %bitcast.3), custom_call_target="tpu_custom_call" | custom-call | tf_op jit(solution)/shard_map/infonce_backward/pallas_call | solution.py:380
  56.2 0.6 %copy.8 = f32[128,128]{1,0:T(8,128)} copy(f32[128,128]{1,0:T(8,128)S(1)} %get-tuple-element.4) | data formatting | bytes 131072
  56.8 0.6 %copy.9 = f32[128,128]{1,0:T(8,128)} copy(f32[128,128]{1,0:T(8,128)S(1)} %get-tuple-element.5) | data formatting | bytes 131072
Async XLA Ops:
  0.6 0.7 %copy-start.2 = (bf16[128]{0:T(256)(128)(2,1)S(1)}, bf16[128]{0:T(256)(128)(2,1)}, u32[]{:S(2)}) copy-start(bf16[128]{0:T(256)(128)(2,1)} %param.6) | copy-start | bytes 772
  0.6 0.7 %copy-start.3 = (bf16[128]{0:T(256)(128)(2,1)S(1)}, bf16[128]{0:T(256)(128)(2,1)}, u32[]{:S(2)}) copy-start(bf16[128]{0:T(256)(128)(2,1)} %param.7) | copy-start | bytes 772
  1.3 0.8 %copy-start = (bf16[128,128]{1,0:T(8,128)(2,1)S(1)}, bf16[128,128]{1,0:T(8,128)(2,1)}, u32[]{:S(2)}) copy-start(bf16[128,128]{1,0:T(8,128)(2,1)} %a_ref.1) | copy-start | bytes 98308
  2.1 0.8 %copy-start.1 = (bf16[128,128]{1,0:T(8,128)(2,1)S(1)}, bf16[128,128]{1,0:T(8,128)(2,1)}, u32[]{:S(2)}) copy-start(bf16[128,128]{1,0:T(8,128)(2,1)} %p_ref.1) | copy-start | bytes 98308

commit v3 on v2

--- a/solution.py
+++ b/solution.py
@@ -56,8 +56,9 @@
     keys += [("p", i) for i in range(1, COLUMNS)]
     keys += [("a", i) for i in range(1, ROWS)]
     keys += [("core", j, dy) for j in (0, 1) for dy in range(NUM_Y)]
-    keys += [("y", j, dy) for j in (0, 1) for dy in range(1, NUM_Y)]
-    keys += [("z",)]
+    keys += [("z", dy % NUM_Y) for dy in (-2, -1, 0, 1, 2)]
+    keys += [("pair", dy % NUM_Y) for dy in (3, 4, -3)]
+    keys += [("y", dy) for dy in range(1, NUM_Y)]
     keys += [("x", dz, dx) for dz in range(NUM_ZH) for dx in range(1, NUM_X)]
     keys += [("zh", dz) for dz in range(1, NUM_ZH)]
     return {key: i for i, key in enumerate(keys)}
@@ -94,6 +95,7 @@
     sibling = row_dev(zl, y, 1 - core)
     z_pair = row_dev(1 - zl, y, core)
     y_dev = {d: row_dev(zl, (y + d) % NUM_Y, core) for d in range(1, NUM_Y)}
+    pair_dev = {d: row_dev(1 - zl, (y + d) % NUM_Y, core) for d in range(1, NUM_Y)}
     x_dev = {d: col_dev(zh, (x + d) % NUM_X) for d in range(1, NUM_X)}
     zh_dev = {d: col_dev((zh + d) % NUM_ZH, x) for d in range(1, NUM_ZH)}
 
@@ -137,19 +139,34 @@
         for d in (1, -1, 2):
             send_a(as_(dz, 0), as_(dz, -d), x_dev[d % NUM_X])
 
-    def p_along_y(j, ds):
+    def p_along_y(ds):
         for d in ds:
-            send_p(ps(j, 0, 0), ps(j, -d, 0), y_dev[d % NUM_Y])
+            send_p(ps(0, 0, 0), ps(0, -d, 0), y_dev[d % NUM_Y])
 
     def to_sibling(j, dy):
         send_p(ps(j, dy, 0), ps(j, dy, 1), sibling)
 
-    def onward(j, s):
-        got_p(j, -2 * s, 0)
-        send_p(ps(j, -2 * s, 0), ps(j, -3 * s, 0), y_dev[s % NUM_Y])
-        if (s > 0) == (j == 0):
-            send_p(ps(j, -2 * s, 0), ps(j, 4, 0), y_dev[2 * s % NUM_Y])
-        to_sibling(j, -2 * s)
+    def to_pair(dy):
+        send_p(ps(0, dy, 0), ps(1, dy, 0), z_pair)
+
+    def spread(dy):
+        got_p(0, dy, 0)
+        to_pair(dy)
+        to_sibling(0, dy)
+
+    def from_pair(dy):
+        got_p(1, dy, 0)
+        to_sibling(1, dy)
+
+    def onward():
+        for s in (1, -1):
+            got_p(0, -2 * s, 0)
+            send_p(ps(0, -2 * s, 0), ps(0, -3 * s, 0), y_dev[s % NUM_Y])
+        source = jnp.where(core == 0, ps(0, -2, 0), ps(0, 2, 0))
+        send_p(source, ps(0, 4, 0), row_dev(zl, (y + jnp.where(core == 0, 2, 6)) % NUM_Y, core))
+        for s in (1, -1):
+            to_pair(-2 * s)
+            to_sibling(0, -2 * s)
 
     def prepare_a(dz):
         first, count = a_slots(dz)
@@ -216,16 +233,24 @@
     def chip_sum(j, dy):
         return own_p(j, dy, 0) + arrived("core", j, dy % NUM_Y)
 
-    def y_sums(*names):
+    def z_sums(*names):
         for name in names:
             for j, dy in P_GROUPS[name]:
-                send_sum(("y", j, dy % NUM_Y), chip_sum(j, dy), y_dev[dy % NUM_Y])
-
-    def y_total(j):
-        total = chip_sum(j, 0)
-        for dy in range(1, NUM_Y):
-            total += arrived("y", j, dy)
-        return total
+                if j == 1:
+                    send_sum(("z", dy % NUM_Y), chip_sum(1, dy), z_pair)
+
+    def pair_far_sums():
+        for j, dy in P_GROUPS["pair_far"]:
+            send_sum(("pair", dy % NUM_Y), chip_sum(j, dy), pair_dev[dy % NUM_Y])
+
+    def pair_sum(dy):
+        if dy in (3, -3, 4):
+            return chip_sum(0, dy)
+        return chip_sum(0, dy) + arrived("z", dy % NUM_Y)
+
+    def y_sums(name):
+        for _, dy in P_GROUPS[name]:
+            send_sum(("y", dy % NUM_Y), pair_sum(dy), y_dev[dy % NUM_Y])
 
     def x_sums(dz):
         for dx in (2, 1, -1):
@@ -240,42 +265,42 @@
     def zh_sum(dz):
         send_sum(("zh", dz % NUM_ZH), x_total(dz), zh_dev[dz % NUM_ZH])
 
-    def diagonal():
-        for dz, dx in A_KEYS:
-            i = as_(dz, dx)
-            other = (zh + dz) % NUM_ZH * NUM_X + (x + dx) % NUM_X
-            j, dy, kk = (core + zl) % 2, (other // 2 + NUM_Y - y) % NUM_Y, (other + core) % 2
-            place = jnp.where(dy <= 3, 2 * dy, 15 - 2 * dy)
-            k = jnp.where(
-                place == 0, 2 * j,
-                jnp.where(
-                    place <= 2, 4 + 8 * j + 2 * (place - 1),
-                    jnp.where(place <= 4, 8 + 14 * j + 2 * (place - 3), 16 + 10 * j + 2 * (place - 5)),
-                ),
-            ) + kk
-            rows, cols = slice(i * BLOCK, (i + 1) * BLOCK), pl.ds(pl.multiple_of(k * BLOCK, BLOCK), BLOCK)
-            acc_a[rows, :] -= 2.0 * pb[k, :BLOCK, :].astype(f32)
-            acc_p[:, cols] -= 2.0 * at[:, rows].astype(f32)
+    def diagonal(*names):
+        for name in names:
+            for j, dy in P_GROUPS[name]:
+
+                @pl.when((c == r // 2) & ((core + zl) % 2 == j))
+                def _():
+                    for kk in (0, 1):
+                        k = ps(j, dy, kk)
+                        other = (y + dy + NUM_Y) % NUM_Y * 2 + (core + kk) % 2
+                        dz, dx = (other // NUM_X + NUM_ZH - zh) % NUM_ZH, (other % NUM_X + NUM_X - x) % NUM_X
+                        i = NUM_X * jnp.where(dz <= 1, 2 * dz, 7 - 2 * dz) + jnp.where(dx <= 1, 2 * dx, 7 - 2 * dx)
+                        rows = pl.ds(pl.multiple_of(i * BLOCK, BLOCK), BLOCK)
+                        cols = slice(k * BLOCK, (k + 1) * BLOCK)
+                        acc_a[rows, :] -= 2.0 * pb[k, :BLOCK, :].astype(f32)
+                        acc_p[:, cols] -= 2.0 * at[:, rows].astype(f32)
+
+    def sums_of(*names):
+        diagonal(*names)
+        core_sums(*names)
 
     send_a(as_(0, 0), as_(-1, 0), zh_dev[1])
     send_a(as_(0, 0), as_(1, 0), zh_dev[3])
-    send_p(ps(0, 0, 0), ps(1, 0, 0), z_pair)
-    p_along_y(0, (1, -1))
+    p_along_y((2, -2, 1, -1))
+    to_pair(0)
     a_along_x(0)
-    p_along_y(0, (2, -2))
     to_sibling(0, 0)
 
-    got_p(1, 0, 0)
-    p_along_y(1, (1, -1, 2, -2))
-    to_sibling(1, 0)
-    for s in (1, -1):
-        got_p(0, s, 0)
-        to_sibling(0, s)
+    for s in (1, -1):
+        spread(s)
+    from_pair(0)
     got_a(-1, 0)
     send_a(as_(-1, 0), as_(2, 0), zh_dev[1])
     a_along_x(-1)
     got_a(1, 0)
     a_along_x(1)
+    onward()
     for d in (1, -1, 2):
         got_a(0, d)
     prepare_a(0)
@@ -283,99 +308,96 @@
         got_p(0, s, 1)
     prepare_p("near")
     tile(a_slots(0), p_slots("near"))
-
-    onward(0, 1)
-    onward(0, -1)
     for s in (1, -1):
         got_p(0, 2 * s, 1)
     prepare_p("next")
     tile(a_slots(0), p_slots("next"))
-
-    for s in (1, -1):
-        got_p(1, s, 0)
-        to_sibling(1, s)
+    for s in (1, -1):
+        from_pair(s)
     got_a(2, 0)
     a_along_x(2)
-    for dz in (-1, 1):
-        for d in (1, -1, 2):
-            got_a(dz, d)
-        prepare_a(dz)
-        tile(a_slots(dz), p_slots("near", "next"))
-        if dz == -1:
-            onward(1, 1)
-            onward(1, -1)
-            for d in (3, -3, 4):
-                got_p(0, d, 0)
-                to_sibling(0, d)
+    for d in (1, -1, 2):
+        got_a(-1, d)
+    prepare_a(-1)
+    tile(a_slots(-1), p_slots("near", "next"))
+    for s in (1, -1):
+        from_pair(2 * s)
+    for d in (3, -3, 4):
+        spread(d)
+    for d in (1, -1, 2):
+        got_a(1, d)
+    prepare_a(1)
+    tile(a_slots(1), p_slots("near", "next"))
     for s in (1, -1):
         got_p(1, s, 1)
     prepare_p("pair_near")
     tile(a_slots(0, -1, 1), p_slots("pair_near"))
-
+    for d in (3, -3, 4):
+        from_pair(d)
     for d in (1, -1, 2):
         got_a(2, d)
     prepare_a(2)
     tile(a_slots(2), p_slots("near", "next", "pair_near"))
-
+    sums_of("pair_near", "next", "near")
+
+    for s in (1, -1):
+        got_p(1, 2 * s, 1)
+    prepare_p("pair_next")
+    tile(a_slots(0, -1, 1, 2), p_slots("pair_next"))
+    sums_of("pair_next")
+    z_sums("pair_near")
     for d in (3, -3, 4):
-        got_p(1, d, 0)
-        to_sibling(1, d)
+        got_p(1, d, 1)
+    prepare_p("pair_far")
+    tile(a_slots(0, -1, 1, 2), p_slots("pair_far"))
+    sums_of("pair_far")
+    z_sums("pair_next")
     for d in (3, -3, 4):
         got_p(0, d, 1)
     prepare_p("far")
-    for d in (2, -2):
-        got_p(1, d, 1)
-    prepare_p("pair_next")
-    for d in (3, -3, 4):
-        got_p(1, d, 1)
-    prepare_p("pair_far")
     got_p(0, 0, 1)
     got_p(1, 0, 1)
     prepare_p("home")
+    tile(a_slots(2), p_slots("far"))
     tile(a_slots(2), p_slots("home"))
-    tile(a_slots(2), p_slots("far", "pair_next", "pair_far"))
-
-    @pl.when(c == r // 2)
-    def _():
-        diagonal()
-
-    core_sums("near", "next", "pair_near")
+    diagonal("far", "home")
     x_sums(2)
-    others = a_slots(0, -1, 1)
-    tile(others, p_slots("far"))
-    core_sums("far")
-    y_sums("near", "next", "pair_near")
-    tile(others, p_slots("pair_far"))
-    core_sums("pair_far")
-    y_sums("far")
-    zh_sum(2)
-    tile(others, p_slots("pair_next"))
-    core_sums("pair_next")
-    y_sums("pair_far")
+    y_sums("near")
+    pair_far_sums()
+    tile(a_slots(-1), p_slots("far"))
     tile(a_slots(-1), p_slots("home"))
     x_sums(-1)
-    y_sums("pair_next")
+    y_sums("next")
+    tile(a_slots(1), p_slots("far"))
     tile(a_slots(1), p_slots("home"))
     x_sums(1)
+    tile(a_slots(0), p_slots("far"))
+    core_sums("far")
+    zh_sum(2)
     tile(a_slots(0), p_slots("home"))
     core_sums("home")
     x_sums(0)
+    y_sums("far")
     zh_sum(-1)
+    z_sums("home")
     zh_sum(1)
-    send_sum(("z",), y_total(1), z_pair)
+    total_p = pair_sum(0)
+    for dy in (1, -1, 2, -2, 3, -3, 4):
+        total_p += arrived("y", dy % NUM_Y)
+    for dy in (3, -3, 4):
+        total_p += arrived("pair", dy % NUM_Y)
+    dp_out[...] = 5.0 * total_p.T
     total_a = x_total(0)
-    for dz in (2, 1, 3):
+    for dz in (2, 3, 1):
         total_a += arrived("zh", dz)
     da_out[...] = 5.0 * total_a
-    total_p = y_total(0) + arrived("z")
-    dp_out[...] = 5.0 * total_p.T
     for copy in copies.values():
         copy.wait_send()
 
 
 def on_device(anchors, positives, row_lse, column_logsumexp):
     vmem = pl.BlockSpec(memory_space=pltpu.VMEM)
-    anywhere = pl.BlockSpec(memory_space=pl.ANY)
+    anywhere = pl.BlockSpec(memory_space=pltpu.HBM)
     block = jax.ShapeDtypeStruct((BLOCK, WIDTH), f32)
     return pl.pallas_call(
         kernel,
@@ -397,7 +419,7 @@
             pltpu.SemaphoreType.DMA((2,)),
         ],
         compiler_params=pltpu.CompilerParams(
-            collective_id=0, has_side_effects=True, vmem_limit_bytes=48 * 2**20
+            collective_id=0, has_side_effects=True, vmem_limit_bytes=63 * 2**20
         ),
         name="infonce_backward",
     )(anchors, positives, row_lse.reshape(1, BLOCK), column_logsumexp.reshape(1, BLOCK))

time: 57.7 us -> 54.1 us (0.938)
  Pallas kernels: 53.4 us -> 51 us
  local copies, waits for them, and re-layouts: 3.43 us -> 2.14 us
    pallas_call x1, Pallas kernels: 53.4 us -> 51 us  [on_device(): pl.pallas_call(kernel, out_shape=(block, block), in_specs=[anywhere, anyw...]
    unnamed x10 -> x4, local copies, waits for them, and re-layouts: 3.43 us -> 2.14 us
where the time goes in v3:
time: 54.1 us; the launch traced here: 53.8 us
  Pallas kernels  51 us (94%)
  local copies, waits for them, and re-layouts  2.14 us (4%)
  between operations  0.65 us (1%)
    pallas_call x1, Pallas kernels, on_device(): pl.pallas_call(kernel, out_shape=(block, block), in_specs=[anywhere, anyw...  51 us
    unnamed x4, local copies, waits for them, and re-layouts  2.14 us

profile of v3, /device:TPU:1, one launch (start us, length us, event | category | flops | bytes accessed | tf_op | source)
XLA Modules:
  0.0 53.8 jit_solution(17056506270794983920)
XLA Ops:
  0.6 51.0 %infonce_backward.1 = (f32[128,128]{1,0:T(8,128)}, f32[128,128]{1,0:T(8,128)}) custom-call(bf16[128,128]{1,0:T(8,128)(2,1)} %a_ref.1, bf16[128,128]{1,0:T(8,128)(2,1)} %p_ref.1, bf16[1,128]{1,0:T(2,128)(2,1)} %bitcast.2, bf16[1,128]{1,0:T(2,128)(2,1)} %bitcast.3), custom_call_target="tpu_custom_call" | custom-call | tf_op jit(solution)/shard_map/infonce_backward/pallas_call | solution.py:402
  51.7 0.0 copy-start
  51.7 1.5 %copy.8 = f32[128,128]{1,0:T(8,128)} copy(f32[128,128]{1,0:T(8,128)} %get-tuple-element.4) | data formatting | bytes 131072
  53.2 0.0 copy-done
  53.2 0.6 %copy.9 = f32[128,128]{1,0:T(8,128)} copy(f32[128,128]{1,0:T(8,128)S(1)} %copy-done) | data formatting | bytes 131072
Async XLA Ops:
  51.7 1.5 %copy-start = (f32[128,128]{1,0:T(8,128)S(1)}, f32[128,128]{1,0:T(8,128)}, u32[]{:S(2)}) copy-start(f32[128,128]{1,0:T(8,128)} %get-tuple-element.5) | copy-start | bytes 196612

commit v4 on v3

--- a/solution.py
+++ b/solution.py
@@ -73,11 +73,13 @@
 
 def kernel(
     a_ref, p_ref, la_ref, lp_ref, da_out, dp_out,
-    ab, pb, at, ub, vb, acc_a, acc_p, out_s, in_s, send_sem, recv_sem, load_sem,
+    ab, pb, at, ub, vb, acc_a, acc_p, out_s, in_s, la, lp, send_sem, recv_sem, load_sem,
 ):
     loads = [
         pltpu.make_async_copy(a_ref, ab.at[0, pl.ds(0, BLOCK)], load_sem.at[0]),
         pltpu.make_async_copy(p_ref, pb.at[0, pl.ds(0, BLOCK)], load_sem.at[1]),
+        pltpu.make_async_copy(la_ref, la, load_sem.at[2]),
+        pltpu.make_async_copy(lp_ref, lp, load_sem.at[3]),
     ]
     for load in loads:
         load.start()
@@ -104,10 +106,10 @@
     barrier = pltpu.get_barrier_semaphore()
     for dev in peers:
         pl.semaphore_signal(barrier, inc=1, device_id=dev, device_id_type=MESH)
-    ab[0, BLOCK:, :] = jnp.broadcast_to(la_ref[...], (SENT - BLOCK, WIDTH))
-    pb[0, BLOCK:, :] = jnp.broadcast_to(lp_ref[...], (SENT - BLOCK, WIDTH))
     for load in loads:
         load.wait()
+    ab[0, BLOCK:, :] = jnp.broadcast_to(la[...], (SENT - BLOCK, WIDTH))
+    pb[0, BLOCK:, :] = jnp.broadcast_to(lp[...], (SENT - BLOCK, WIDTH))
     pl.semaphore_wait(barrier, len(peers))
 
     copies = {}
@@ -172,7 +174,7 @@
         first, count = a_slots(dz)
         for i in range(first, first + count):
             rows = slice(i * BLOCK, (i + 1) * BLOCK)
-            at[:, rows] = ab[i, :BLOCK, :].astype(f32).T.astype(bf16)
+            at[:, rows] = ab[i, :BLOCK, :].T
             lse = ab[i, BLOCK:, :].astype(f32)[0:1, :]
             ub[rows, :] = jnp.broadcast_to(jnp.exp(TOP - lse), (BLOCK, BLOCK)).T
 
@@ -367,19 +369,19 @@
     tile(a_slots(-1), p_slots("far"))
     tile(a_slots(-1), p_slots("home"))
     x_sums(-1)
-    y_sums("next")
     tile(a_slots(1), p_slots("far"))
     tile(a_slots(1), p_slots("home"))
     x_sums(1)
+    y_sums("next")
     tile(a_slots(0), p_slots("far"))
     core_sums("far")
-    zh_sum(2)
     tile(a_slots(0), p_slots("home"))
     core_sums("home")
     x_sums(0)
     y_sums("far")
+    z_sums("home")
+    zh_sum(2)
     zh_sum(-1)
-    z_sums("home")
     zh_sum(1)
     total_p = pair_sum(0)
     for dy in (1, -1, 2, -2, 3, -3, 4):
@@ -402,7 +404,7 @@
     return pl.pallas_call(
         kernel,
         out_shape=(block, block),
-        in_specs=[anywhere, anywhere, vmem, vmem],
+        in_specs=[anywhere] * 4,
         out_specs=(vmem, vmem),
         scratch_shapes=[
             pltpu.VMEM((ROWS, SENT, WIDTH), bf16),
@@ -414,9 +416,11 @@
             pltpu.VMEM((WIDTH, COLUMNS * BLOCK), f32),
             pltpu.VMEM((len(SUM_KEYS), BLOCK, WIDTH), bf16),
             pltpu.VMEM((len(SUM_KEYS), BLOCK, WIDTH), bf16),
+            pltpu.VMEM((1, BLOCK), bf16),
+            pltpu.VMEM((1, BLOCK), bf16),
             pltpu.SemaphoreType.DMA((len(SEM),)),
             pltpu.SemaphoreType.DMA((len(SEM),)),
-            pltpu.SemaphoreType.DMA((2,)),
+            pltpu.SemaphoreType.DMA((4,)),
         ],
         compiler_params=pltpu.CompilerParams(
             collective_id=0, has_side_effects=True, vmem_limit_bytes=63 * 2**20

time: 54.1 us -> 53.4 us (0.987)
  Pallas kernels: 51 us -> 50.3 us
    pallas_call x1, Pallas kernels: 51 us -> 50.3 us  [on_device(): pl.pallas_call(kernel, out_shape=(block, block), in_specs=[anywhere] * 4,...]
where the time goes in v4:
time: 53.4 us; the launch traced here: 53.1 us
  Pallas kernels  50.3 us (94%)
  local copies, waits for them, and re-layouts  2.14 us (4%)
  between operations  0.65 us (1%)
    pallas_call x1, Pallas kernels, on_device(): pl.pallas_call(kernel, out_shape=(block, block), in_specs=[anywhere] * 4,...  50.3 us
    unnamed x4, local copies, waits for them, and re-layouts  2.14 us

profile of v4, /device:TPU:1, one launch (start us, length us, event | category | flops | bytes accessed | tf_op | source)
XLA Modules:
  0.0 53.1 jit_solution(4077768659905148996)
XLA Ops:
  0.6 50.3 %infonce_backward.1 = (f32[128,128]{1,0:T(8,128)}, f32[128,128]{1,0:T(8,128)}) custom-call(bf16[128,128]{1,0:T(8,128)(2,1)} %a_ref.1, bf16[128,128]{1,0:T(8,128)(2,1)} %p_ref.1, bf16[1,128]{1,0:T(2,128)(2,1)} %bitcast.2, bf16[1,128]{1,0:T(2,128)(2,1)} %bitcast.3), custom_call_target="tpu_custom_call" | custom-call | tf_op jit(solution)/shard_map/infonce_backward/pallas_call | solution.py:404
  51.0 0.0 copy-start
  51.0 1.5 %copy.8 = f32[128,128]{1,0:T(8,128)} copy(f32[128,128]{1,0:T(8,128)} %get-tuple-element.4) | data formatting | bytes 131072
  52.5 0.0 copy-done
  52.5 0.6 %copy.9 = f32[128,128]{1,0:T(8,128)} copy(f32[128,128]{1,0:T(8,128)S(1)} %copy-done) | data formatting | bytes 131072
Async XLA Ops:
  51.0 1.5 %copy-start = (f32[128,128]{1,0:T(8,128)S(1)}, f32[128,128]{1,0:T(8,128)}, u32[]{:S(2)}) copy-start(f32[128,128]{1,0:T(8,128)} %get-tuple-element.5) | copy-start | bytes 196612

commit v5 on v4

--- a/solution.py
+++ b/solution.py
@@ -423,10 +423,13 @@
             pltpu.SemaphoreType.DMA((4,)),
         ],
         compiler_params=pltpu.CompilerParams(
-            collective_id=0, has_side_effects=True, vmem_limit_bytes=63 * 2**20
+            collective_id=0, has_side_effects=True, vmem_limit_bytes=48 * 2**20
         ),
         name="infonce_backward",
-    )(anchors, positives, row_lse.reshape(1, BLOCK), column_logsumexp.reshape(1, BLOCK))
+    )(*(
+        pltpu.with_memory_space_constraint(value, pltpu.HBM)
+        for value in (anchors, positives, row_lse.reshape(1, BLOCK), column_logsumexp.reshape(1, BLOCK))
+    ))
 
 
 def solution(mesh):

time: 53.4 us -> 51.8 us (0.970)
  local copies, waits for them, and re-layouts: 2.14 us -> 1.26 us
  Pallas kernels: 50.3 us -> 49.7 us
    unnamed x4 -> x2, local copies, waits for them, and re-layouts: 2.14 us -> 1.26 us
    pallas_call x1, Pallas kernels: 50.3 us -> 49.7 us  [on_device(): pl.pallas_call(kernel, out_shape=(block, block), in_specs=[anywhere] * 4,...]
where the time goes in v5:
time: 51.8 us; the launch traced here: 51.6 us
  Pallas kernels  49.7 us (96%)
  local copies, waits for them, and re-layouts  1.26 us (2%)
  between operations  0.64 us (1%)
    pallas_call x1, Pallas kernels, on_device(): pl.pallas_call(kernel, out_shape=(block, block), in_specs=[anywhere] * 4,...  49.7 us
    unnamed x2, local copies, waits for them, and re-layouts  1.26 us

profile of v5, /device:TPU:1, one launch (start us, length us, event | category | flops | bytes accessed | tf_op | source)
XLA Modules:
  0.0 51.6 jit_solution(15317399034724219543)
XLA Ops:
  0.6 49.7 %infonce_backward.1 = (f32[128,128]{1,0:T(8,128)S(1)}, f32[128,128]{1,0:T(8,128)S(1)}) custom-call(bf16[128,128]{1,0:T(8,128)(2,1)} %a_ref.1, bf16[128,128]{1,0:T(8,128)(2,1)} %p_ref.1, bf16[1,128]{1,0:T(2,128)(2,1)} %bitcast.2, bf16[1,128]{1,0:T(2,128)(2,1)} %bitcast.3), custom_call_target="tpu_custom_call" | custom-call | tf_op jit(solution)/shard_map/infonce_backward/pallas_call | solution.py:404
  50.3 0.6 %copy.8 = f32[128,128]{1,0:T(8,128)} copy(f32[128,128]{1,0:T(8,128)S(1)} %get-tuple-element.4) | data formatting | bytes 131072
  51.0 0.6 %copy.9 = f32[128,128]{1,0:T(8,128)} copy(f32[128,128]{1,0:T(8,128)S(1)} %get-tuple-element.5) | data formatting | bytes 131072
